TPU v7x, 256 devices: a whole 4x4x8 slice. The times are simulated.
256 devices in a mesh: pp: 4 (over y), node: 8 (over x, core), local: 8 (over z).
Axes of the slice: x: 4, y: 4, z: 8, core: 2. Of those that a mesh axis runs over, the one named last changes fastest.
Arguments:
- act_fwd: bfloat16 [4, 8192, 4096], P('pp', ('node', 'local')), may hold values from -6 to 6
- routes_fwd: int32 [4, 8192, 1], P('pp', ('node', 'local')), may hold values from 0 to 7; in each aligned block of 128 rows (0 to 127, 128 to 255, ..., all dimensions but the last counted through in order) at most 20 rows name the same one
- weight_fwd: float32 [4, 8192], P('pp', ('node', 'local')), may hold values from 0.25 to 1
- grad_bwd: bfloat16 [4, 8192, 4096], P('pp', ('node', 'local')), may hold values from -6 to 6
- routes_bwd: int32 [4, 8192, 1], P('pp', ('node', 'local')), may hold values from 0 to 7; in each aligned block of 128 rows (0 to 127, 128 to 255, ..., all dimensions but the last counted through in order) at most 20 rows name the same one
- weight_bwd: float32 [4, 8192], P('pp', ('node', 'local')), may hold values from 0.25 to 1
- saved_bwd: bfloat16 [4, 8192, 2048], P('pp', ('node', 'local')), may hold values from -8 to 8
- w_gate_up: bfloat16 [4, 8, 4096, 2048], P('pp', 'node', 'local'), may hold values from -0.09375 to 0.09375
- w_down: bfloat16 [4, 8, 1024, 4096], P('pp', 'node', None, 'local'), may hold values from -0.1875 to 0.1875
Outputs:
- next_input: bfloat16 [4, 8192, 4096], P('pp', ('node', 'local'))
- prev_grad: bfloat16 [4, 8192, 4096], P('pp', ('node', 'local'))
Inputs may be any that keep to these rules, and one draw needn't show every extreme that they name: `routes_fwd`: within each device's 128 tokens (aligned blocks of rows), no expert is named more than 20 times, a bound that some block reaches. `routes_bwd`: within each device's 128 tokens (aligned blocks of rows), no expert is named more than 20 times, a bound that some block reaches.
All inputs are finite; a program needn't handle non-finite values.
Results may differ from a plain program's by a relative error of at most 0.017.
Values may be sent and summed in bfloat16 or wider, within the bound.
A program may use at most 128 MiB of HBM per device.

v0:
```python
import jax
import jax.numpy as jnp
from jax import lax
from jax.sharding import PartitionSpec as P


def place_matrix(route, expert_count, capacity):
    rows = route.shape[0]
    same = route[:, None] == route[None, :]
    earlier = (
        jnp.arange(rows, dtype=jnp.int32)[None, :] < jnp.arange(rows, dtype=jnp.int32)[:, None]
    )
    slot_index = jnp.sum((same & earlier).astype(jnp.int32), axis=1)
    target = route * capacity + slot_index
    positions = jnp.arange(expert_count * capacity, dtype=jnp.int32)
    return (positions[:, None] == target[None, :]).astype(jnp.bfloat16)


def pack_rows(placer, values):
    return jnp.dot(placer, values, preferred_element_type=jnp.float32).astype(jnp.bfloat16)


def unpack_rows(placer, packed):
    return lax.dot_general(
        placer, packed, (((0,), (0,)), ((), ())), preferred_element_type=jnp.float32
    )


def swap(packed, nodes):
    blocks = packed.reshape(nodes, -1, packed.shape[1])
    return lax.all_to_all(blocks, "node", split_axis=0, concat_axis=0, tiled=True).reshape(
        packed.shape
    )


def body(
    act_fwd, routes_fwd, weight_fwd, grad_bwd, routes_bwd, weight_bwd, saved_bwd, w_gate_up, w_down
):
    nodes = lax.axis_size("node")
    capacity = 5 * act_fwd.shape[1] // (4 * nodes)
    w_gu = lax.all_gather(w_gate_up[0, 0], "local", axis=0, tiled=True)
    w_dn = lax.all_gather(w_down[0, 0], "local", axis=0, tiled=False)
    shards, hidden_units, column = w_dn.shape
    tokens = act_fwd[0]
    cotangent = grad_bwd[0]
    placer_a = place_matrix(routes_fwd[0, :, 0], nodes, capacity)
    placer_b = place_matrix(routes_bwd[0, :, 0], nodes, capacity)
    scaled = (weight_bwd[0][:, None] * cotangent.astype(jnp.float32)).astype(jnp.bfloat16)
    rows_a = swap(pack_rows(placer_a, tokens), nodes)
    rows_b = swap(pack_rows(placer_b, scaled), nodes)
    saved = swap(pack_rows(placer_b, saved_bwd[0]), nodes)
    grad_hidden = sum(
        (
            lax.dot_general(
                rows_b[:, j * column : (j + 1) * column],
                w_dn[j],
                (((1,), (1,)), ((), ())),
                preferred_element_type=jnp.float32,
            )
            for j in range(shards)
        )
    )
    gate_pre = saved[:, :hidden_units].astype(jnp.float32)
    up_pre = saved[:, hidden_units:].astype(jnp.float32)
    sigmoid_g = 1.0 / (1.0 + jnp.exp(-gate_pre))
    grad_gate = grad_hidden * up_pre * sigmoid_g * (1.0 + gate_pre * (1.0 - sigmoid_g))
    grad_up = grad_hidden * gate_pre * sigmoid_g
    grad_gu = jnp.concatenate([grad_gate, grad_up], axis=1).astype(jnp.bfloat16)
    done_b = lax.dot_general(
        grad_gu, w_gu, (((1,), (1,)), ((), ())), preferred_element_type=jnp.float32
    ).astype(jnp.bfloat16)
    preact = jnp.dot(rows_a, w_gu, preferred_element_type=jnp.float32)
    hidden = (jax.nn.silu(preact[:, :hidden_units]) * preact[:, hidden_units:]).astype(jnp.bfloat16)
    done_a = jnp.concatenate(
        [
            jnp.dot(hidden, w_dn[j], preferred_element_type=jnp.float32).astype(jnp.bfloat16)
            for j in range(shards)
        ],
        axis=1,
    )
    moe_a = unpack_rows(placer_a, swap(done_a, nodes))
    moe_b = unpack_rows(placer_b, swap(done_b, nodes))
    result_a = (tokens.astype(jnp.float32) + weight_fwd[0][:, None] * moe_a).astype(jnp.bfloat16)
    result_b = (cotangent.astype(jnp.float32) + moe_b).astype(jnp.bfloat16)
    length = lax.axis_size("pp")
    next_input = lax.ppermute(result_a[None], "pp", [(i, (i + 1) % length) for i in range(length)])
    prev_grad = lax.ppermute(result_b[None], "pp", [(i, (i - 1) % length) for i in range(length)])
    return (next_input, prev_grad)


def solution(mesh):
    in_specs = (
        P("pp", ("node", "local"), None),
        P("pp", ("node", "local"), None),
        P("pp", ("node", "local")),
        P("pp", ("node", "local"), None),
        P("pp", ("node", "local"), None),
        P("pp", ("node", "local")),
        P("pp", ("node", "local"), None),
        P("pp", "node", "local", None),
        P("pp", "node", None, "local"),
    )
    out_specs = (P("pp", ("node", "local"), None), P("pp", ("node", "local"), None))
    return jax.shard_map(body, mesh=mesh, in_specs=in_specs, out_specs=out_specs, check_vma=False)
```

profile of v0, /device:TPU:1, one launch (start us, length us, event | category | flops | bytes accessed | tf_op | source)
XLA Modules:
  0.0 383.1 jit_solution(13642669705079317526)
XLA Ops:
  10.2 7.3 %all-to-all-start.3 = ((bf16[8,20,2048]{2,1,0:T(8,128)(2,1)}), bf16[8,20,2048]{2,1,0:T(8,128)(2,1)}, u32[]{:S(2)}, u32[]{:S(2)}) async-start(bf16[8,20,2048]{2,1,0:T(8,128)(2,1)} %reshape.64), calls=%async_computation.3 | async-start | bytes 1572864 | tf_op jit(solution)/shard_map/all_to_all | solution.py:31
  19.5 10.5 %all-to-all-done.3 = bf16[8,20,2048]{2,1,0:T(8,128)(2,1)} async-done(((bf16[8,20,2048]{2,1,0:T(8,128)(2,1)}), bf16[8,20,2048]{2,1,0:T(8,128)(2,1)}, u32[]{:S(2)}, u32[]{:S(2)}) %all-to-all-start.3) | async-done | bytes 655392 | tf_op jit(solution)/shard_map/all_to_all | solution.py:31
  30.0 4.4 %all-to-all-start.2 = ((bf16[8,20,4096]{2,1,0:T(8,128)(2,1)}), bf16[8,20,4096]{2,1,0:T(8,128)(2,1)S(1)}, u32[]{:S(2)}, u32[]{:S(2)}) async-start(bf16[8,20,4096]{2,1,0:T(8,128)(2,1)} %reshape.62), calls=%async_computation.2 | async-start | bytes 3145728 | tf_op jit(solution)/shard_map/all_to_all | solution.py:31
  34.5 1.7 convolution_convert_fusion.1
  37.6 17.4 %all-to-all-done.2 = bf16[8,20,4096]{2,1,0:T(8,128)(2,1)S(1)} async-done(((bf16[8,20,4096]{2,1,0:T(8,128)(2,1)}), bf16[8,20,4096]{2,1,0:T(8,128)(2,1)S(1)}, u32[]{:S(2)}, u32[]{:S(2)}) %all-to-all-start.2) | async-done | bytes 1310752 | tf_op jit(solution)/shard_map/all_to_all | solution.py:31
  55.1 5.0 %all-to-all-start = ((bf16[8,20,4096]{2,1,0:T(8,128)(2,1)}), bf16[8,20,4096]{2,1,0:T(8,128)(2,1)}, u32[]{:S(2)}, u32[]{:S(2)}) async-start(bf16[8,20,4096]{2,1,0:T(8,128)(2,1)} %reshape.58), calls=%async_computation | async-start | bytes 3145728 | tf_op jit(solution)/shard_map/all_to_all | solution.py:31
  60.1 2.0 reshape.65
  62.4 18.5 %all-to-all-done = bf16[8,20,4096]{2,1,0:T(8,128)(2,1)} async-done(((bf16[8,20,4096]{2,1,0:T(8,128)(2,1)}), bf16[8,20,4096]{2,1,0:T(8,128)(2,1)}, u32[]{:S(2)}, u32[]{:S(2)}) %all-to-all-start) | async-done | bytes 1310752 | tf_op jit(solution)/shard_map/all_to_all | solution.py:31
  82.5 25.3 %all-gather.7.cloned.1.call-done = bf16[8,1,1024,512]{3,2,1,0:T(8,128)(2,1)} async-done(((bf16[1,1,1024,512]{3,2,1,0:T(8,128)(2,1)}), bf16[8,1,1024,512]{3,2,1,0:T(8,128)(2,1)}) %all-gather.7.cloned.1.call-update) | async-done | bytes 8388624 | tf_op jit(solution)/shard_map/all_gather | solution.py:42
  107.8 1.9 fusion.25
  109.6 2.1 convolution_add_fusion.7
  111.8 1.7 convolution_add_fusion.6
  113.5 1.7 convolution_add_fusion.5
  118.7 162.3 %all-gather.5.cloned.1.call-done = bf16[1,1,4096,2048]{3,2,1,0:T(8,128)(2,1)} async-done(((bf16[1,1,512,2048]{3,2,1,0:T(8,128)(2,1)}), bf16[1,1,4096,2048]{3,2,1,0:T(8,128)(2,1)}) %all-gather.5.cloned.1.call-update) | async-done | bytes 16777232 | tf_op jit(solution)/shard_map/all_gather | solution.py:41
  281.0 11.6 %fusion.5 = bf16[160,4096]{1,0:T(8,128)(2,1)S(1)} fusion(bf16[1,1,4096,2048]{3,2,1,0:T(8,128)(2,1)} %all-gather.5.cloned.1.call-done, bf16[160,1024]{1,0:T(8,128)(2,1)} %get-tuple-element.3, bf16[160,1024]{1,0:T(8,128)(2,1)S(1)} %get-tuple-element.2), kind=kOutput, calls=%fused_computation.7 | convolution fusion | flops 2686320640 | bytes 18743296 | tf_op jit(solution)/shard_map/dot_general | solution.py:69
  293.9 4.9 %all-to-all-start.4 = ((bf16[8,20,4096]{2,1,0:T(8,128)(2,1)}), bf16[8,20,4096]{2,1,0:T(8,128)(2,1)S(1)}, u32[]{:S(2)}, u32[]{:S(2)}) async-start(bf16[8,20,4096]{2,1,0:T(8,128)(2,1)} %reshape.66), calls=%async_computation.4 | async-start | bytes 3145728 | tf_op jit(solution)/shard_map/all_to_all | solution.py:31
  298.8 7.3 %fusion.2 = f32[160,2048]{1,0:T(8,128)S(1)} fusion(bf16[160,4096]{1,0:T(8,128)(2,1)S(1)} %reshape.59, bf16[1,1,4096,2048]{3,2,1,0:T(8,128)(2,1)} %all-gather.5.cloned.1.call-done), kind=kOutput, calls=%fused_computation.2 | convolution fusion | flops 2684354560 | bytes 19398656 | tf_op jit(solution)/shard_map/dot_general | solution.py:72
  320.2 4.8 %all-to-all-start.1 = ((bf16[8,20,4096]{2,1,0:T(8,128)(2,1)}), bf16[8,20,4096]{2,1,0:T(8,128)(2,1)}, u32[]{:S(2)}, u32[]{:S(2)}) async-start(bf16[8,20,4096]{2,1,0:T(8,128)(2,1)} %reshape.60), calls=%async_computation.1 | async-start | bytes 3145728 | tf_op jit(solution)/shard_map/all_to_all | solution.py:31
  325.3 2.7 fusion.10
  328.0 2.5 collective-permute-start.1
  330.5 15.4 %all-to-all-done.1 = bf16[8,20,4096]{2,1,0:T(8,128)(2,1)} async-done(((bf16[8,20,4096]{2,1,0:T(8,128)(2,1)}), bf16[8,20,4096]{2,1,0:T(8,128)(2,1)}, u32[]{:S(2)}, u32[]{:S(2)}) %all-to-all-start.1) | async-done | bytes 1310752 | tf_op jit(solution)/shard_map/all_to_all | solution.py:31
  349.2 4.2 %collective-permute-done.1 = bf16[1,128,4096]{2,1,0:T(8,128)(2,1)} collective-permute-done((bf16[1,128,4096]{2,1,0:T(8,128)(2,1)}, bf16[1,128,4096]{2,1,0:T(8,128)(2,1)}, u32[]{:S(2)}, u32[]{:S(2)}) %collective-permute-start.1) | collective-permute-done | bytes 1048608 | tf_op jit(solution)/shard_map/ppermute | solution.py:87
  353.4 19.6 %collective-permute-done = bf16[1,128,4096]{2,1,0:T(8,128)(2,1)S(1)} collective-permute-done((bf16[1,128,4096]{2,1,0:T(8,128)(2,1)S(1)}, bf16[1,128,4096]{2,1,0:T(8,128)(2,1)S(1)}, u32[]{:S(2)}, u32[]{:S(2)}) %collective-permute-start) | collective-permute-done | bytes 1048608 | tf_op jit(solution)/shard_map/ppermute | solution.py:86
  374.0 2.3 copy.21
  (56 shorter events, 31.6 us)
Async XLA Ops:
  7.2 1.7 copy-start
  7.2 100.6 %all-gather.7.cloned.1.call-start = ((), (), s32[]{:S(2)}) async-start(), calls=%async_computation.6 | async-start | bytes 9437184 | tf_op jit(solution)/shard_map/all_gather | solution.py:42
  7.9 0.8 copy-start.8
  7.9 273.0 %all-gather.5.cloned.1.call-start = ((), (), s32[]{:S(2)}) async-start(), calls=%async_computation.5 | async-start | bytes 18874368 | tf_op jit(solution)/shard_map/all_gather | solution.py:41
  9.2 8.4 %copy-start.4 = (bf16[1,128,4096]{2,1,0:T(8,128)(2,1)S(1)}, bf16[1,128,4096]{2,1,0:T(8,128)(2,1)}, u32[]{:S(2)}) copy-start(bf16[1,128,4096]{2,1,0:T(8,128)(2,1)} %param.12) | copy-start | bytes 3145732
  9.2 8.4 %copy-start.7 = (f32[1,128]{1,0:T(1,128)S(1)}, f32[1,128]{1,0:T(1,128)}, u32[]{:S(2)}) copy-start(f32[1,128]{1,0:T(1,128)} %param.14) | copy-start | bytes 1540
  10.2 19.7 %all-to-all-start.3 = ((bf16[8,20,2048]{2,1,0:T(8,128)(2,1)}), bf16[8,20,2048]{2,1,0:T(8,128)(2,1)}, u32[]{:S(2)}, u32[]{:S(2)}) async-start(bf16[8,20,2048]{2,1,0:T(8,128)(2,1)} %reshape.64), calls=%async_computation.3 | async-start | bytes 1572864 | tf_op jit(solution)/shard_map/all_to_all | solution.py:31
  19.5 14.9 %copy-start.9 = (s32[1,128,1]{1,2,0:T(1,128)S(1)}, s32[1,128,1]{1,2,0:T(1,128)}, u32[]{:S(2)}) copy-start(s32[1,128,1]{1,2,0:T(1,128)} %param.10) | copy-start | bytes 1540
  30.0 25.1 %all-to-all-start.2 = ((bf16[8,20,4096]{2,1,0:T(8,128)(2,1)}), bf16[8,20,4096]{2,1,0:T(8,128)(2,1)S(1)}, u32[]{:S(2)}, u32[]{:S(2)}) async-start(bf16[8,20,4096]{2,1,0:T(8,128)(2,1)} %reshape.62), calls=%async_computation.2 | async-start | bytes 3145728 | tf_op jit(solution)/shard_map/all_to_all | solution.py:31
  55.1 25.9 %all-to-all-start = ((bf16[8,20,4096]{2,1,0:T(8,128)(2,1)}), bf16[8,20,4096]{2,1,0:T(8,128)(2,1)}, u32[]{:S(2)}, u32[]{:S(2)}) async-start(bf16[8,20,4096]{2,1,0:T(8,128)(2,1)} %reshape.58), calls=%async_computation | async-start | bytes 3145728 | tf_op jit(solution)/shard_map/all_to_all | solution.py:31
  107.8 7.4 %copy-start.2 = (bf16[8,1,1024,512]{3,2,1,0:T(8,128)(2,1)S(1)}, bf16[8,1,1024,512]{3,2,1,0:T(8,128)(2,1)}, u32[]{:S(2)}) copy-start(bf16[8,1,1024,512]{3,2,1,0:T(8,128)(2,1)} %all-gather.7.cloned.1.call-done) | copy-start | bytes 25165828
  116.2 1.1 copy-start.5
  293.9 26.3 %all-to-all-start.4 = ((bf16[8,20,4096]{2,1,0:T(8,128)(2,1)}), bf16[8,20,4096]{2,1,0:T(8,128)(2,1)S(1)}, u32[]{:S(2)}, u32[]{:S(2)}) async-start(bf16[8,20,4096]{2,1,0:T(8,128)(2,1)} %reshape.66), calls=%async_computation.4 | async-start | bytes 3145728 | tf_op jit(solution)/shard_map/all_to_all | solution.py:31
  320.2 25.6 %all-to-all-start.1 = ((bf16[8,20,4096]{2,1,0:T(8,128)(2,1)}), bf16[8,20,4096]{2,1,0:T(8,128)(2,1)}, u32[]{:S(2)}, u32[]{:S(2)}) async-start(bf16[8,20,4096]{2,1,0:T(8,128)(2,1)} %reshape.60), calls=%async_computation.1 | async-start | bytes 3145728 | tf_op jit(solution)/shard_map/all_to_all | solution.py:31
  328.0 19.4 %copy-start.3 = (bf16[1,128,4096]{2,1,0:T(8,128)(2,1)S(1)}, bf16[1,128,4096]{2,1,0:T(8,128)(2,1)}, u32[]{:S(2)}) copy-start(bf16[1,128,4096]{2,1,0:T(8,128)(2,1)} %param.9) | copy-start | bytes 3145732
  328.0 19.4 %copy-start.6 = (f32[1,128]{1,0:T(1,128)S(1)}, f32[1,128]{1,0:T(1,128)}, u32[]{:S(2)}) copy-start(f32[1,128]{1,0:T(1,128)} %param.11) | copy-start | bytes 1540
  328.0 25.4 %collective-permute-start.1 = (bf16[1,128,4096]{2,1,0:T(8,128)(2,1)}, bf16[1,128,4096]{2,1,0:T(8,128)(2,1)}, u32[]{:S(2)}, u32[]{:S(2)}) collective-permute-start(bf16[1,128,4096]{2,1,0:T(8,128)(2,1)} %fusion.10), channel_id=1, source_target_pairs={{0,192},{64,0},{128,64},{192,128},{1,193},{65,1},{129,65},{193,129... | collective-permute-start | bytes 3145736 | tf_op jit(solution)/shard_map/ppermute | solution.py:87
  347.9 25.1 %collective-permute-start = (bf16[1,128,4096]{2,1,0:T(8,128)(2,1)S(1)}, bf16[1,128,4096]{2,1,0:T(8,128)(2,1)S(1)}, u32[]{:S(2)}, u32[]{:S(2)}) collective-permute-start(bf16[1,128,4096]{2,1,0:T(8,128)(2,1)S(1)} %fusion.11), channel_id=1, source_target_pairs={{0,64},{64,128},{128,192},{192,0},{1,65},{65,129},{129,193},{193,1... | collective-permute-start | bytes 3145736 | tf_op jit(solution)/shard_map/ppermute | solution.py:86
  373.0 3.3 copy-start.1
Sparse Core Ops, SparseCore 0:
  9.8 97.9 all-gather.6
  109.6 171.3 all-gather.4
where the time goes:
time: 384 us; the launch traced here: 383 us
  waiting for transfers between devices  275 us (72%)
  matrix products  47.5 us (12%)
  starting transfers between devices  30.3 us (8%)
  local copies, waits for them, and re-layouts  15.9 us (4%)
  between operations  14.3 us (4%)
    all_gather x1, waiting for transfers between devices, body(): w_gu = lax.all_gather(w_gate_up[0, 0], 'local', axis=0, tiled=True)  162 us
    all_to_all x5, waiting for transfers between devices, swap(): lax.all_to_all(blocks, 'node', split_axis=0, concat_axis=0, tiled=True)  61.8 us
    all_to_all x5, starting transfers between devices, swap(): lax.all_to_all(blocks, 'node', split_axis=0, concat_axis=0, tiled=True)  26.4 us
    all_gather x1, waiting for transfers between devices, body(): w_dn = lax.all_gather(w_down[0, 0], 'local', axis=0, tiled=False)  25.3 us
    ppermute x1, waiting for transfers between devices, body(): lax.ppermute(result_a[None], 'pp', [(i, (i + 1) % length) for i in range(...  19.6 us
    dot_general x8, matrix products, body(): jnp.dot(hidden, w_dn[j], preferred_element_type=jnp.float32)  12.5 us
    dot_general x1, matrix products, body(): lax.dot_general(grad_gu, w_gu, (((1,), (1,)), ((), ())), preferred_elemen...  11.6 us
    dot_general x8, matrix products, body(): lax.dot_general(rows_b[:, j * column:(j + 1) * column], w_dn[j], (((1,),...  10.3 us
  transfers between devices with their start and end apart: 9, of which 8 were waited for; matrix products, arithmetic and copies ran while one was open for 12% of the time, Pallas kernels for 0%

commit v1 on v0

--- a/solution.py
+++ b/solution.py
@@ -38,7 +38,9 @@
 ):
     nodes = lax.axis_size("node")
     capacity = 5 * act_fwd.shape[1] // (4 * nodes)
-    w_gu = lax.all_gather(w_gate_up[0, 0], "local", axis=0, tiled=True)
+    w_gu = jnp.concatenate(
+        lax.all_to_all(jnp.stack([w_gate_up[0, 0]] * lax.axis_size("local")), "local", 0, 0), axis=0
+    )
     w_dn = lax.all_gather(w_down[0, 0], "local", axis=0, tiled=False)
     shards, hidden_units, column = w_dn.shape
     tokens = act_fwd[0]

time: 384 us -> 650 us (1.69)
  waiting for transfers between devices: 275 us -> 500 us
  blocking collectives: 0 us -> 26 us
    all_gather x1, waiting for transfers between devices: 25.3 us -> 302 us  [body(): w_dn = lax.all_gather(w_down[0, 0], 'local', axis=0, tiled=False)]
    all_gather x1 -> x0, waiting for transfers between devices: 162 us -> none  [body(): w_gu = lax.all_gather(w_gate_up[0, 0], 'local', axis=0, tiled=True)]
    all_to_all x0 -> x1, waiting for transfers between devices: none -> 126 us  [body(): lax.all_to_all(jnp.stack([w_gate_up[0, 0]] * lax.axis_size('local')), 'lo...]
    all_to_all x0 -> x1, blocking collectives: none -> 26 us  [swap(): lax.all_to_all(blocks, 'node', split_axis=0, concat_axis=0, tiled=True)]
    ppermute x1, waiting for transfers between devices: 19.6 us -> 3.95 us  [body(): lax.ppermute(result_a[None], 'pp', [(i, (i + 1) % length) for i in range(...]
    ppermute x1, waiting for transfers between devices: 4.18 us -> 17.6 us  [body(): lax.ppermute(result_b[None], 'pp', [(i, (i - 1) % length) for i in range(...]
    all_to_all x5 -> x4, waiting for transfers between devices: 61.8 us -> 49.4 us  [swap(): lax.all_to_all(blocks, 'node', split_axis=0, concat_axis=0, tiled=True)]
    all_to_all x0 -> x1, starting transfers between devices: none -> 6.64 us  [body(): lax.all_to_all(jnp.stack([w_gate_up[0, 0]] * lax.axis_size('local')), 'lo...]
  transfers between devices with their start and end apart: 9 -> 8, of which waited for: 8 -> 8; matrix products, arithmetic and copies ran while one was open for 12% -> 7% of each run, Pallas kernels for 0% -> 0%
where the time goes in v1:
time: 650 us; the launch traced here: 648 us
  waiting for transfers between devices  500 us (77%)
  matrix products  52.7 us (8%)
  starting transfers between devices  31.7 us (5%)
  blocking collectives  26 us (4%)
  local copies, waits for them, and re-layouts  21.6 us (3%)
  between operations  14.3 us (2%)
    all_gather x1, waiting for transfers between devices, body(): w_dn = lax.all_gather(w_down[0, 0], 'local', axis=0, tiled=False)  302 us
    all_to_all x1, waiting for transfers between devices, body(): lax.all_to_all(jnp.stack([w_gate_up[0, 0]] * lax.axis_size('local')), 'lo...  126 us
    all_to_all x4, waiting for transfers between devices, swap(): lax.all_to_all(blocks, 'node', split_axis=0, concat_axis=0, tiled=True)  49.4 us
    all_to_all x1, blocking collectives, swap(): lax.all_to_all(blocks, 'node', split_axis=0, concat_axis=0, tiled=True)  26 us
    all_to_all x4, starting transfers between devices, swap(): lax.all_to_all(blocks, 'node', split_axis=0, concat_axis=0, tiled=True)  20.9 us
    ppermute x1, waiting for transfers between devices, body(): lax.ppermute(result_b[None], 'pp', [(i, (i - 1) % length) for i in range(...  17.6 us
    dot_general x8, matrix products, body(): lax.dot_general(rows_b[:, j * column:(j + 1) * column], w_dn[j], (((1,),...  15.5 us
  transfers between devices with their start and end apart: 8, of which 8 were waited for; matrix products, arithmetic and copies ran while one was open for 7% of the time, Pallas kernels for 0%

profile of v1, /device:TPU:1, one launch (start us, length us, event | category | flops | bytes accessed | tf_op | source)
XLA Modules:
  0.0 648.0 jit_solution(16609217558110996981)
XLA Ops:
  10.1 7.3 %all-to-all-start.4 = ((bf16[8,20,2048]{2,1,0:T(8,128)(2,1)}), bf16[8,20,2048]{2,1,0:T(8,128)(2,1)}, u32[]{:S(2)}, u32[]{:S(2)}) async-start(bf16[8,20,2048]{2,1,0:T(8,128)(2,1)} %reshape.70), calls=%async_computation.4 | async-start | bytes 1572864 | tf_op jit(solution)/shard_map/all_to_all | solution.py:31
  19.4 10.4 %all-to-all-done.4 = bf16[8,20,2048]{2,1,0:T(8,128)(2,1)} async-done(((bf16[8,20,2048]{2,1,0:T(8,128)(2,1)}), bf16[8,20,2048]{2,1,0:T(8,128)(2,1)}, u32[]{:S(2)}, u32[]{:S(2)}) %all-to-all-start.4) | async-done | bytes 655392 | tf_op jit(solution)/shard_map/all_to_all | solution.py:31
  29.9 4.4 all-to-all-start
  34.2 1.8 convolution_convert_fusion.1
  37.4 17.6 %all-to-all-done = bf16[8,20,4096]{2,1,0:T(8,128)(2,1)S(1)} async-done(((bf16[8,20,4096]{2,1,0:T(8,128)(2,1)}), bf16[8,20,4096]{2,1,0:T(8,128)(2,1)S(1)}, u32[]{:S(2)}, u32[]{:S(2)}) %all-to-all-start) | async-done | bytes 1310752 | tf_op jit(solution)/shard_map/all_to_all | solution.py:31
  55.0 26.0 %all_to_all.30 = bf16[8,20,4096]{2,1,0:T(8,128)(2,1)} all-to-all(bf16[8,20,4096]{2,1,0:T(8,128)(2,1)} %reshape.68), channel_id=1, replica_groups=mesh['pp'=4,'node'=8,'local'=8] {'node'}, dimensions={0} | all-to-all | bytes 2621440 | tf_op jit(solution)/shard_map/all_to_all | solution.py:31
  81.0 6.0 stack.3
  87.0 6.6 %all-to-all-start.1 = ((bf16[8,512,2048]{2,1,0:T(8,128)(2,1)}), bf16[8,512,2048]{2,1,0:T(8,128)(2,1)}, u32[]{:S(2)}, u32[]{:S(2)}) async-start(bf16[8,512,2048]{2,1,0:T(8,128)(2,1)} %stack.3), calls=%async_computation.1 | async-start | bytes 33554432 | tf_op jit(solution)/shard_map/all_to_all | solution.py:42
  94.3 2.0 reshape.71
  98.2 302.5 %all-gather.3.cloned.1.call-done = bf16[8,1,1024,512]{3,2,1,0:T(8,128)(2,1)} async-done(((bf16[1,1,1024,512]{3,2,1,0:T(8,128)(2,1)}), bf16[8,1,1024,512]{3,2,1,0:T(8,128)(2,1)}) %all-gather.3.cloned.1.call-update) | async-done | bytes 8388624 | tf_op jit(solution)/shard_map/all_gather | solution.py:44
  411.0 2.6 convolution_add_fusion.2
  413.5 125.7 %all-to-all-done.1 = bf16[8,512,2048]{2,1,0:T(8,128)(2,1)} async-done(((bf16[8,512,2048]{2,1,0:T(8,128)(2,1)}), bf16[8,512,2048]{2,1,0:T(8,128)(2,1)}, u32[]{:S(2)}, u32[]{:S(2)}) %all-to-all-start.1) | async-done | bytes 16777248 | tf_op jit(solution)/shard_map/all_to_all | solution.py:42
  539.2 7.3 %fusion.48 = f32[160,2048]{1,0:T(8,128)S(1)} fusion(bf16[160,4096]{1,0:T(8,128)(2,1)S(1)} %reshape.64, bf16[4096,2048]{1,0:T(8,128)(2,1)} %bitcast.4), kind=kOutput, calls=%fused_computation.88 | convolution fusion | flops 2684354560 | bytes 19398656 | tf_op jit(solution)/shard_map/dot_general | solution.py:74
  560.6 4.2 all-to-all-start.2
  564.8 2.7 fusion.24
  567.5 11.6 %convolution_convert_fusion = bf16[160,4096]{1,0:T(8,128)(2,1)S(1)} fusion(bf16[4096,2048]{1,0:T(8,128)(2,1)} %bitcast.4, bf16[160,1024]{1,0:T(8,128)(2,1)} %get-tuple-element.3, bf16[160,1024]{1,0:T(8,128)(2,1)S(1)} %get-tuple-element.2), kind=kOutput, calls=%fused_computation.3 | convolution fusion | flops 2686320640 | bytes 18743296 | tf_op jit(solution)/shard_map/dot_general | solution.py:71
  580.4 5.2 all-to-all-done.2
  585.5 5.0 all-to-all-start.5
  591.2 2.7 fusion.4
  595.2 16.2 %all-to-all-done.5 = bf16[8,20,4096]{2,1,0:T(8,128)(2,1)} async-done(((bf16[8,20,4096]{2,1,0:T(8,128)(2,1)}), bf16[8,20,4096]{2,1,0:T(8,128)(2,1)}, u32[]{:S(2)}, u32[]{:S(2)}) %all-to-all-start.5) | async-done | bytes 1310752 | tf_op jit(solution)/shard_map/all_to_all | solution.py:31
  613.4 2.8 collective-permute-start.1
  616.3 4.0 collective-permute-done
  620.2 17.6 %collective-permute-done.1 = bf16[1,128,4096]{2,1,0:T(8,128)(2,1)S(1)} collective-permute-done((bf16[1,128,4096]{2,1,0:T(8,128)(2,1)S(1)}, bf16[1,128,4096]{2,1,0:T(8,128)(2,1)S(1)}, u32[]{:S(2)}, u32[]{:S(2)}) %collective-permute-start.1) | collective-permute-done | bytes 1048608 | tf_op jit(solution)/shard_map/ppermute | solution.py:89
  637.9 2.3 copy.20
  (57 shorter events, 39.4 us)
Async XLA Ops:
  7.2 1.6 copy-start
  9.1 8.4 %copy-start.10 = (s32[1,128,1]{1,2,0:T(1,128)S(1)}, s32[1,128,1]{1,2,0:T(1,128)}, u32[]{:S(2)}) copy-start(s32[1,128,1]{1,2,0:T(1,128)} %param.10) | copy-start | bytes 1540
  9.1 8.5 %copy-start.3 = (bf16[1,128,4096]{2,1,0:T(8,128)(2,1)S(1)}, bf16[1,128,4096]{2,1,0:T(8,128)(2,1)}, u32[]{:S(2)}) copy-start(bf16[1,128,4096]{2,1,0:T(8,128)(2,1)} %param.9) | copy-start | bytes 3145732
  10.1 19.7 %all-to-all-start.4 = ((bf16[8,20,2048]{2,1,0:T(8,128)(2,1)}), bf16[8,20,2048]{2,1,0:T(8,128)(2,1)}, u32[]{:S(2)}, u32[]{:S(2)}) async-start(bf16[8,20,2048]{2,1,0:T(8,128)(2,1)} %reshape.70), calls=%async_computation.4 | async-start | bytes 1572864 | tf_op jit(solution)/shard_map/all_to_all | solution.py:31
  19.4 14.8 %copy-start.9 = (f32[1,128]{1,0:T(1,128)S(1)}, f32[1,128]{1,0:T(1,128)}, u32[]{:S(2)}) copy-start(f32[1,128]{1,0:T(1,128)} %param.14) | copy-start | bytes 1540
  29.9 25.1 %all-to-all-start = ((bf16[8,20,4096]{2,1,0:T(8,128)(2,1)}), bf16[8,20,4096]{2,1,0:T(8,128)(2,1)S(1)}, u32[]{:S(2)}, u32[]{:S(2)}) async-start(bf16[8,20,4096]{2,1,0:T(8,128)(2,1)} %reshape.63), calls=%async_computation | async-start | bytes 3145728 | tf_op jit(solution)/shard_map/all_to_all | solution.py:31
  55.0 26.1 %copy-start.5 = (bf16[1,1,512,2048]{3,2,1,0:T(8,128)(2,1)S(1)}, bf16[1,1,512,2048]{3,2,1,0:T(8,128)(2,1)}, u32[]{:S(2)}) copy-start(bf16[1,1,512,2048]{3,2,1,0:T(8,128)(2,1)} %param.16) | copy-start | bytes 6291460
  87.0 452.2 %all-to-all-start.1 = ((bf16[8,512,2048]{2,1,0:T(8,128)(2,1)}), bf16[8,512,2048]{2,1,0:T(8,128)(2,1)}, u32[]{:S(2)}, u32[]{:S(2)}) async-start(bf16[8,512,2048]{2,1,0:T(8,128)(2,1)} %stack.3), calls=%async_computation.1 | async-start | bytes 33554432 | tf_op jit(solution)/shard_map/all_to_all | solution.py:42
  93.6 307.1 %all-gather.3.cloned.1.call-start = ((), (), s32[]{:S(2)}) async-start(), calls=%async_computation.6 | async-start | bytes 9437184 | tf_op jit(solution)/shard_map/all_gather | solution.py:44
  98.2 312.8 %copy-start.2 = (bf16[160,4096]{1,0:T(8,128)(2,1)}, bf16[160,4096]{1,0:T(8,128)(2,1)S(1)}, u32[]{:S(2)}) copy-start(bf16[160,4096]{1,0:T(8,128)(2,1)S(1)} %reshape.69) | copy-start | bytes 3932164
  560.6 4.2 copy-start.6
  560.6 4.2 copy-start.7
  560.6 24.9 %all-to-all-start.2 = ((bf16[8,20,4096]{2,1,0:T(8,128)(2,1)}), bf16[8,20,4096]{2,1,0:T(8,128)(2,1)S(1)}, u32[]{:S(2)}, u32[]{:S(2)}) async-start(bf16[8,20,4096]{2,1,0:T(8,128)(2,1)} %reshape.66), calls=%async_computation.2 | async-start | bytes 3145728 | tf_op jit(solution)/shard_map/all_to_all | solution.py:31
  585.5 25.9 %all-to-all-start.5 = ((bf16[8,20,4096]{2,1,0:T(8,128)(2,1)}), bf16[8,20,4096]{2,1,0:T(8,128)(2,1)}, u32[]{:S(2)}, u32[]{:S(2)}) async-start(bf16[8,20,4096]{2,1,0:T(8,128)(2,1)} %reshape.72), calls=%async_computation.5 | async-start | bytes 3145728 | tf_op jit(solution)/shard_map/all_to_all | solution.py:31
  590.6 0.7 copy-start.8
  593.9 19.0 %copy-start.4 = (bf16[1,128,4096]{2,1,0:T(8,128)(2,1)S(1)}, bf16[1,128,4096]{2,1,0:T(8,128)(2,1)}, u32[]{:S(2)}) copy-start(bf16[1,128,4096]{2,1,0:T(8,128)(2,1)} %param.12) | copy-start | bytes 3145732
  593.9 26.3 %collective-permute-start = (bf16[1,128,4096]{2,1,0:T(8,128)(2,1)}, bf16[1,128,4096]{2,1,0:T(8,128)(2,1)}, u32[]{:S(2)}, u32[]{:S(2)}) collective-permute-start(bf16[1,128,4096]{2,1,0:T(8,128)(2,1)} %fusion.4), channel_id=1, source_target_pairs={{0,64},{64,128},{128,192},{192,0},{1,65},{65,129},{129,193},{193,1... | collective-permute-start | bytes 3145736 | tf_op jit(solution)/shard_map/ppermute | solution.py:88
  613.4 24.4 %collective-permute-start.1 = (bf16[1,128,4096]{2,1,0:T(8,128)(2,1)S(1)}, bf16[1,128,4096]{2,1,0:T(8,128)(2,1)S(1)}, u32[]{:S(2)}, u32[]{:S(2)}) collective-permute-start(bf16[1,128,4096]{2,1,0:T(8,128)(2,1)S(1)} %fusion.3), channel_id=1, source_target_pairs={{0,192},{64,0},{128,64},{192,128},{1,193},{65,1},{129,65},{193,129... | collective-permute-start | bytes 3145736 | tf_op jit(solution)/shard_map/ppermute | solution.py:89
  637.9 3.3 copy-start.1
Sparse Core Ops, SparseCore 0:
  96.2 304.3 all-gather.2
